TPU v7x, 32 devices: a whole 2x2x4 slice. The times are simulated.
32 devices in a mesh: ctx: 8 (over z, y), head: 4 (over x, core).
Axes of the slice: x: 2, y: 2, z: 4, core: 2. Of those that a mesh axis runs over, the one named last changes fastest.
Arguments:
- tokens: bfloat16 [3072, 3840], P(('ctx', 'head'))
- w_query: bfloat16 [3840, 4096], P(None, 'head')
- w_key: bfloat16 [3840, 2048], P(None, 'head')
- w_value: bfloat16 [3840, 2048], P(None, 'head'), may hold values from -0.09375 to 0.09375
- query_gain: float32 [256], replicated
- key_gain: float32 [256], replicated
- positions: int32 [3072], P('ctx'), may hold values from 0 to 3071, as said below
- out_grad: bfloat16 [3072, 4096], P('ctx', 'head'), may hold values from -6 to 6
Outputs:
- attended: bfloat16 [3072, 4096], P('ctx', 'head')
- input_grad: bfloat16 [3072, 3840], P(('ctx', 'head'))
- grad_query: bfloat16 [3840, 4096], P('ctx', 'head')
- grad_key: bfloat16 [3840, 2048], P('ctx', 'head')
- grad_value: bfloat16 [3840, 2048], P('ctx', 'head')
Inputs may be any that keep to these rules, and one draw needn't show every extreme that they name: `positions`: positions rise by one from token to token inside a document and are 0 at a document's first token; the window's first document began before the window; no document that starts inside the window is longer than 2048 tokens.
All inputs are finite; a program needn't handle non-finite values.
Results may differ from a plain program's by a relative error of at most 0.04.
The roundings to bfloat16 on the way count: a program that leaves them out, or rounds other values in their place, can miss the bound.
Values may be sent and summed in bfloat16 or wider, within the bound.
A program may use at most 192 MiB of HBM per device.

v0:
```python
from functools import reduce
import math

import jax
import jax.numpy as jnp
from jax import lax
from jax.sharding import PartitionSpec as P

WINDOW = 1024


norm_eps = 1e-06
rope_base = 10000.0


def passed_along(block, axis, distance):
    devices = range(lax.axis_size(axis))
    route = [(i - distance, i) for i in devices if i - distance in devices]
    return lax.ppermute(block, axis, route)


def rope_tables(positions, head_width):
    half_width = head_width // 2
    indices = jnp.arange(half_width, dtype=jnp.float32)
    frequency = jnp.power(rope_base, -2.0 * indices / head_width)
    angles = positions.astype(jnp.float32)[:, None] * frequency[None, :]
    return (jnp.cos(angles)[:, None, :], jnp.sin(angles)[:, None, :])


def rotate(vector, cosine_table, sine_table):
    half_width = vector.shape[-1] // 2
    lower_half = vector[..., :half_width]
    upper_half = vector[..., half_width:]
    return jnp.concatenate(
        [
            lower_half * cosine_table - upper_half * sine_table,
            upper_half * cosine_table + lower_half * sine_table,
        ],
        axis=-1,
    )


def unrotate(rotated, cosine_table, sine_table):
    half_width = rotated.shape[-1] // 2
    lower_half = rotated[..., :half_width]
    upper_half = rotated[..., half_width:]
    return jnp.concatenate(
        [
            lower_half * cosine_table + upper_half * sine_table,
            upper_half * cosine_table - lower_half * sine_table,
        ],
        axis=-1,
    )


def normalize(vector, gain_vector):
    inv_rms = lax.rsqrt(jnp.mean(vector * vector, axis=-1, keepdims=True) + norm_eps)
    return (vector * inv_rms * gain_vector, inv_rms)


def norm_back(vector, inv_rms, gain_vector, upstream):
    scaled = upstream * gain_vector
    return inv_rms * scaled - vector * (inv_rms * inv_rms * inv_rms) * jnp.mean(
        vector * scaled, axis=-1, keepdims=True
    )


def on_device(tokens, w_query, w_key, w_value, query_gain, key_gain, positions, out_grad):
    gathered = lax.all_gather(tokens, "head", axis=0, tiled=True)
    row_count = gathered.shape[0]
    head_width = query_gain.shape[0]
    head_count = w_query.shape[1] // head_width
    groups = w_key.shape[1] // head_width
    group_size = head_count // groups
    rank_count = lax.axis_size("ctx")
    my_rank = lax.axis_index("ctx")
    reach_blocks = min((WINDOW - 2) // row_count + 1, rank_count - 1)
    query_scale = 1.0 / math.sqrt(head_width)
    query_raw = jnp.dot(gathered, w_query, preferred_element_type=jnp.float32).reshape(
        row_count, head_count, head_width
    )
    key_raw = jnp.dot(gathered, w_key, preferred_element_type=jnp.float32).reshape(
        row_count, groups, head_width
    )
    value_states = jnp.dot(gathered, w_value, preferred_element_type=jnp.float32).astype(
        jnp.bfloat16
    )
    cosine_table, sine_table = rope_tables(positions, head_width)
    query_normed, query_inv = normalize(query_raw, query_gain)
    key_normed, key_inv = normalize(key_raw, key_gain)
    query_states = (
        (rotate(query_normed, cosine_table, sine_table) * query_scale)
        .astype(jnp.bfloat16)
        .reshape(row_count, groups, group_size, head_width)
    )
    key_states = (
        rotate(key_normed, cosine_table, sine_table)
        .astype(jnp.bfloat16)
        .reshape(row_count, groups * head_width)
    )
    local_kv = jnp.stack([key_states, value_states])
    blocks = [local_kv]
    moving = local_kv
    for stride in range(reach_blocks):
        moving = passed_along(moving, "ctx", 1)
        blocks.append(moving)
    offsets = jnp.arange(row_count, dtype=jnp.int32)
    reach_limit = jnp.minimum(positions, WINDOW - 1)[:, None]
    visible_sets = []
    live_flags = []
    for stride in range(reach_blocks + 1):
        distance = stride * row_count + offsets[:, None] - offsets[None, :]
        visible = (distance >= 0) & (distance <= reach_limit) & (my_rank >= stride)
        visible_sets.append(visible)
        live_flags.append(jnp.any(visible))

    def block_keys(stride):
        return blocks[stride][0].reshape(row_count, groups, head_width)

    def block_values(stride):
        return blocks[stride][1].reshape(row_count, groups, head_width)

    def score_block(stride):
        return jnp.einsum(
            "qgue,kge->guqk", query_states, block_keys(stride), preferred_element_type=jnp.float32
        )

    scores = [score_block(stride) for stride in range(reach_blocks + 1)]
    row_peak = reduce(
        jnp.maximum,
        [
            jnp.max(
                jnp.where(visible_sets[stride], scores[stride], -jnp.inf), axis=-1, keepdims=True
            )
            for stride in range(reach_blocks + 1)
        ],
    )
    weights = [
        jnp.where(visible_sets[stride], jnp.exp(scores[stride] - row_peak), 0.0)
        for stride in range(reach_blocks + 1)
    ]
    row_total = reduce(
        jnp.add, [jnp.sum(weight_block, axis=-1, keepdims=True) for weight_block in weights]
    )
    probabilities = [weight_block / row_total for weight_block in weights]
    prob_bf16 = [prob_block.astype(jnp.bfloat16) for prob_block in probabilities]

    def mix_values(stride):
        return jnp.einsum(
            "guqk,kge->qgue",
            prob_bf16[stride],
            block_values(stride),
            preferred_element_type=jnp.float32,
        )

    mixed = reduce(jnp.add, [mix_values(stride) for stride in range(reach_blocks + 1)])
    attended = mixed.astype(jnp.bfloat16)
    grad_heads = out_grad.reshape(row_count, groups, group_size, head_width)
    row_delta = jnp.einsum(
        "qgue,qgue->guq", grad_heads, attended, preferred_element_type=jnp.float32
    )[..., None]

    def back_block(stride):
        key_block = block_keys(stride)
        dprobs = jnp.einsum(
            "qgue,kge->guqk", grad_heads, block_values(stride), preferred_element_type=jnp.float32
        )
        dscores = (probabilities[stride] * (dprobs - row_delta)).astype(jnp.bfloat16)
        query_grad = jnp.einsum(
            "guqk,kge->qgue", dscores, key_block, preferred_element_type=jnp.float32
        )
        key_grad = jnp.einsum(
            "guqk,qgue->kge", dscores, query_states, preferred_element_type=jnp.float32
        )
        value_grad = jnp.einsum(
            "guqk,qgue->kge", prob_bf16[stride], grad_heads, preferred_element_type=jnp.float32
        )
        return (
            query_grad,
            jnp.stack(
                [
                    key_grad.reshape(row_count, groups * head_width),
                    value_grad.reshape(row_count, groups * head_width),
                ]
            ),
        )

    back_terms = [back_block(stride) for stride in range(reach_blocks + 1)]
    query_grads = reduce(jnp.add, [term_pair[0] for term_pair in back_terms])
    key_grad_parts = [term_pair[1] for term_pair in back_terms]
    returned = key_grad_parts[reach_blocks]
    for stride in range(reach_blocks, 0, -1):
        returned = (
            passed_along(returned.astype(jnp.bfloat16), "ctx", -1).astype(returned.dtype)
            + key_grad_parts[stride - 1]
        )
    key_grads = returned[0].reshape(row_count, groups, head_width)
    value_grads = returned[1].astype(jnp.bfloat16)
    query_raw_grad = (
        norm_back(
            query_raw,
            query_inv,
            query_gain,
            unrotate(
                query_grads.reshape(row_count, head_count, head_width), cosine_table, sine_table
            )
            * query_scale,
        )
        .astype(jnp.bfloat16)
        .reshape(row_count, head_count * head_width)
    )
    key_raw_grad = (
        norm_back(key_raw, key_inv, key_gain, unrotate(key_grads, cosine_table, sine_table))
        .astype(jnp.bfloat16)
        .reshape(row_count, groups * head_width)
    )
    input_terms = (
        jnp.dot(query_raw_grad, w_query.T, preferred_element_type=jnp.float32)
        + jnp.dot(key_raw_grad, w_key.T, preferred_element_type=jnp.float32)
        + jnp.dot(value_grads, w_value.T, preferred_element_type=jnp.float32)
    )
    input_grad = lax.psum_scatter(
        input_terms.astype(jnp.bfloat16), "head", scatter_dimension=0, tiled=True
    )
    grad_columns = jnp.concatenate([query_raw_grad, key_raw_grad, value_grads], axis=1)
    summed = lax.psum_scatter(
        lax.dot_general(
            gathered, grad_columns, (((0,), (0,)), ((), ())), preferred_element_type=jnp.float32
        ).astype(jnp.bfloat16),
        "ctx",
        scatter_dimension=0,
        tiled=True,
    ).astype(jnp.float32)
    summed = summed.astype(jnp.bfloat16)
    query_cols = head_count * head_width
    key_cols = groups * head_width
    return (
        attended.reshape(row_count, query_cols),
        input_grad,
        summed[:, :query_cols],
        summed[:, query_cols : query_cols + key_cols],
        summed[:, query_cols + key_cols :],
    )


def solution(mesh):
    in_specs = (
        P(("ctx", "head"), None),
        P(None, "head"),
        P(None, "head"),
        P(None, "head"),
        P(),
        P(),
        P("ctx"),
        P("ctx", "head"),
    )
    out_specs = (
        P("ctx", "head"),
        P(("ctx", "head"), None),
        P("ctx", "head"),
        P("ctx", "head"),
        P("ctx", "head"),
    )
    return jax.shard_map(
        on_device, mesh=mesh, in_specs=in_specs, out_specs=out_specs, check_vma=False
    )
```

profile of v0, /device:TPU:0, one launch (start us, length us, event | category | flops | bytes accessed | tf_op | source)
XLA Modules:
  0.0 586.7 jit_solution(17305635078053136294)
XLA Ops:
  15.9 23.9 %all-gather.2.cloned.1.call-done = bf16[384,3840]{1,0:T(8,128)(2,1)} async-done(((bf16[96,3840]{1,0:T(8,128)(2,1)}), bf16[384,3840]{1,0:T(8,128)(2,1)}) %all-gather.2.cloned.1.call-update) | async-done | bytes 2949136 | tf_op jit(solution)/shard_map/all_gather | solution.py:69
  39.7 4.7 fusion.101
  46.6 4.8 convolution_convert_fusion
  52.5 4.3 collective-permute-start
  56.8 7.7 %fusion.102 = f32[384,1024]{1,0:T(8,128)} fusion(bf16[384,3840]{1,0:T(8,128)(2,1)S(1)} %copy-done.72, bf16[3840,1024]{1,0:T(8,128)(2,1)} %param.9), kind=kOutput, calls=%fused_computation.163 | convolution fusion | flops 3019898880 | bytes 12386304 | tf_op jit(solution)/shard_map/dot_general | solution.py:79
  67.7 5.7 collective-permute-done
  73.4 5.4 collective-permute-start.1
  105.3 4.3 collective-permute-start.2
  109.6 3.7 fusion.15
  121.1 3.7 fusion.12
  135.5 3.6 fusion.24
  145.3 4.0 copy.381
  149.4 3.6 multiply_reduce_fusion
  154.7 3.0 fusion.4
  201.7 5.8 collective-permute-done.3
  213.8 14.7 %collective-permute-done.4 = bf16[2,384,512]{2,1,0:T(8,128)(2,1)S(1)} collective-permute-done((bf16[2,384,512]{2,1,0:T(8,128)(2,1)S(1)}, bf16[2,384,512]{2,1,0:T(8,128)(2,1)S(1)}, u32[]{:S(2)}, u32[]{:S(2)}) %collective-permute-start.4) | collective-permute-done | bytes 786464 | tf_op jit(solution)/shard_map/ppermute | solution.py:19
  235.8 3.0 fusion.108
  241.0 4.7 subtract_convert_fusion
  257.2 11.5 %convert_bitcast_fusion = bf16[3840,2048]{0,1:T(8,128)(2,1)} fusion(bf16[384,3840]{1,0:T(8,128)(2,1)S(1)} %copy-done.73, bf16[384,512]{1,0:T(8,128)(2,1)S(1)} %copy-done.62, bf16[384,512]{1,0:T(8,128)(2,1)S(1)} %subtract_convert_fusion.1, bf16[384,1024]{1,0:T(8,128)(2,1)S(1)} %copy-done.54), kind=kOutput, calls=%fused_computation | convolution fusion | flops 6052380672 | bytes 20250624 | tf_op jit(solution)/shard_map/dot_general | solution.py:227
  268.8 20.7 %copy.452 = bf16[3840,2048]{1,0:T(8,128)(2,1)} copy(bf16[3840,2048]{0,1:T(8,128)(2,1)} %convert_bitcast_fusion) | data formatting | bytes 31457280
  289.7 6.0 %fusion.105 = f32[384,3840]{1,0:T(8,128)S(1)} fusion(bf16[384,1024]{1,0:T(8,128)(2,1)S(1)} %copy-done.54, bf16[3840,1024]{1,0:T(8,128)(2,1)} %param.9), kind=kOutput, calls=%fused_computation.166 | convolution fusion | flops 3019898880 | bytes 14548992 | tf_op jit(solution)/shard_map/dot_general | solution.py:218
  298.7 3.4 fusion
  304.4 236.6 %reduce-scatter.7.cloned.1.call-done = bf16[480,2048]{1,0:T(8,128)(2,1)} async-done(((bf16[3840,2048]{1,0:T(8,128)(2,1)}), bf16[480,2048]{1,0:T(8,128)(2,1)}) %reduce-scatter.7.cloned.1.call-update) | async-done | bytes 1966096
  544.4 35.6 %reduce-scatter.5.cloned.1.call-done = bf16[96,3840]{1,0:T(8,128)(2,1)} async-done(((bf16[384,3840]{1,0:T(8,128)(2,1)}), bf16[96,3840]{1,0:T(8,128)(2,1)}) %reduce-scatter.5.cloned.1.call-update) | async-done | bytes 737296 | tf_op jit(solution)/shard_map/reduce_scatter | solution.py:222
  (276 shorter events, 147.6 us)
Async XLA Ops:
  7.2 6.5 %copy-start.71 = (s32[384]{0:T(512)S(1)}, s32[384]{0:T(512)}, u32[]{:S(2)}) copy-start(s32[384]{0:T(512)} %param.14) | copy-start | bytes 4612
  7.2 32.5 %all-gather.2.cloned.1.call-start = ((), (), s32[]{:S(2)}) async-start(), calls=%async_computation.2 | async-start | bytes 3686400 | tf_op jit(solution)/shard_map/all_gather | solution.py:69
  7.9 533.0 %reduce-scatter.7.cloned.1.call-start = ((), (), s32[]{:S(2)}) async-start(), calls=%async_computation.4 | async-start | bytes 17694720
  12.5 27.2 %copy-start.66 = (f32[256]{0:T(256)}, f32[256]{0:T(256)S(1)}, u32[]{:S(2)}) copy-start(f32[256]{0:T(256)S(1)} %broadcast_multiply_fusion.2) | copy-start | bytes 3076
  46.6 10.2 %copy-start.72 = (bf16[384,3840]{1,0:T(8,128)(2,1)S(1)}, bf16[384,3840]{1,0:T(8,128)(2,1)}, u32[]{:S(2)}) copy-start(bf16[384,3840]{1,0:T(8,128)(2,1)} %all-gather.2.cloned.1.call-done) | copy-start | bytes 8847364
  52.5 20.9 %collective-permute-start = (bf16[2,384,512]{2,1,0:T(8,128)(2,1)}, bf16[2,384,512]{2,1,0:T(8,128)(2,1)}, u32[]{:S(2)}, u32[]{:S(2)}) collective-permute-start(bf16[2,384,512]{2,1,0:T(8,128)(2,1)} %pad_maximum_fusion.1), channel_id=1, source_target_pairs={{0,4},{4,8},{8,12},{12,16},{16,20},{20,24},{24,28},{1,5},{5,9},{9,... | collective-permute-start | bytes 2359304 | tf_op jit(solution)/shard_map/ppermute | solution.py:19
  67.2 6.2 %copy-start.37 = (f32[384,4]{1,0:T(8,128)}, f32[384,4]{1,0:T(8,128)S(1)}, u32[]{:S(2)}) copy-start(f32[384,4]{1,0:T(8,128)S(1)} %copy.292) | copy-start | bytes 18436
  73.4 32.0 %collective-permute-start.1 = (bf16[2,384,512]{2,1,0:T(8,128)(2,1)}, bf16[2,384,512]{2,1,0:T(8,128)(2,1)}, u32[]{:S(2)}, u32[]{:S(2)}) collective-permute-start(bf16[2,384,512]{2,1,0:T(8,128)(2,1)} %collective-permute-done), channel_id=1, source_target_pairs={{0,4},{4,8},{8,12},{12,16},{16,20},{20,24},{24,28},{1,5},{5,9},{9,... | collective-permute-start | bytes 2359304 | tf_op jit(solution)/shard_map/ppermute | solution.py:19
  105.3 19.8 %collective-permute-start.2 = (bf16[2,384,512]{2,1,0:T(8,128)(2,1)}, bf16[2,384,512]{2,1,0:T(8,128)(2,1)}, u32[]{:S(2)}, u32[]{:S(2)}) collective-permute-start(bf16[2,384,512]{2,1,0:T(8,128)(2,1)} %collective-permute-done.1), channel_id=1, source_target_pairs={{0,4},{4,8},{8,12},{12,16},{16,20},{20,24},{24,28},{1,5},{5,9},{9,... | collective-permute-start | bytes 2359304 | tf_op jit(solution)/shard_map/ppermute | solution.py:19
  134.7 8.1 %copy-start.7 = (f32[2,384,384,2]{2,1,3,0:T(8,128)}, f32[2,384,384,2]{2,1,3,0:T(8,128)S(1)}, u32[]{:S(2)}) copy-start(f32[2,384,384,2]{2,1,3,0:T(8,128)S(1)} %get-tuple-element.71) | copy-start | bytes 7077892
  157.8 10.2 %copy-start.12 = (bf16[2,2,384,384]{2,3,1,0:T(8,128)(2,1)}, bf16[2,2,384,384]{2,3,1,0:T(8,128)(2,1)S(1)}, u32[]{:S(2)}) copy-start(bf16[2,2,384,384]{2,3,1,0:T(8,128)(2,1)S(1)} %fusion.4) | copy-start | bytes 3538948
  159.9 8.6 %copy-start.11 = (bf16[2,2,384,384]{2,3,1,0:T(8,128)(2,1)}, bf16[2,2,384,384]{2,3,1,0:T(8,128)(2,1)S(1)}, u32[]{:S(2)}) copy-start(bf16[2,2,384,384]{2,3,1,0:T(8,128)(2,1)S(1)} %fusion.8) | copy-start | bytes 3538948
  162.1 7.6 %copy-start.13 = (bf16[2,2,384,384]{2,3,1,0:T(8,128)(2,1)}, bf16[2,2,384,384]{2,3,1,0:T(8,128)(2,1)S(1)}, u32[]{:S(2)}) copy-start(bf16[2,2,384,384]{2,3,1,0:T(8,128)(2,1)S(1)} %fusion.6) | copy-start | bytes 3538948
  186.9 20.6 %collective-permute-start.3 = (bf16[2,384,512]{2,1,0:T(8,128)(2,1)}, bf16[2,384,512]{2,1,0:T(8,128)(2,1)}, u32[]{:S(2)}, u32[]{:S(2)}) collective-permute-start(bf16[2,384,512]{2,1,0:T(8,128)(2,1)} %pad_maximum_fusion.2), channel_id=1, source_target_pairs={{4,0},{8,4},{12,8},{16,12},{20,16},{24,20},{28,24},{5,1},{9,5},{13... | collective-permute-start | bytes 2359304 | tf_op jit(solution)/shard_map/ppermute | solution.py:19
  199.8 7.7 %copy-start.24 = (f32[1,384,512]{2,1,0:T(8,128)S(1)}, f32[1,384,512]{2,1,0:T(8,128)}, u32[]{:S(2)}) copy-start(f32[1,384,512]{2,1,0:T(8,128)} %copy.447) | copy-start | bytes 2359300
  199.8 7.7 %copy-start.25 = (f32[1,384,512]{2,1,0:T(8,128)S(1)}, f32[1,384,512]{2,1,0:T(8,128)}, u32[]{:S(2)}) copy-start(f32[1,384,512]{2,1,0:T(8,128)} %copy.446) | copy-start | bytes 2359300
  201.7 8.6 %copy-start.67 = (f32[256]{0:T(256)S(1)}, f32[256]{0:T(256)}, u32[]{:S(2)}) copy-start(f32[256]{0:T(256)} %copy-done.66) | copy-start | bytes 3076
  209.0 19.5 %collective-permute-start.4 = (bf16[2,384,512]{2,1,0:T(8,128)(2,1)S(1)}, bf16[2,384,512]{2,1,0:T(8,128)(2,1)S(1)}, u32[]{:S(2)}, u32[]{:S(2)}) collective-permute-start(bf16[2,384,512]{2,1,0:T(8,128)(2,1)S(1)} %fusion.30), channel_id=1, source_target_pairs={{4,0},{8,4},{12,8},{16,12},{20,16},{24,20},{28,24},{5,1},{9,5},{13... | collective-permute-start | bytes 2359304 | tf_op jit(solution)/shard_map/ppermute | solution.py:19
  212.2 16.4 %copy-start.20 = (f32[1,384,512]{2,1,0:T(8,128)S(1)}, f32[1,384,512]{2,1,0:T(8,128)}, u32[]{:S(2)}) copy-start(f32[1,384,512]{2,1,0:T(8,128)} %copy.449) | copy-start | bytes 2359300
  212.2 16.4 %copy-start.21 = (f32[1,384,512]{2,1,0:T(8,128)S(1)}, f32[1,384,512]{2,1,0:T(8,128)}, u32[]{:S(2)}) copy-start(f32[1,384,512]{2,1,0:T(8,128)} %copy.448) | copy-start | bytes 2359300
  229.8 18.9 %collective-permute-start.5 = (bf16[2,384,512]{2,1,0:T(8,128)(2,1)}, bf16[2,384,512]{2,1,0:T(8,128)(2,1)}, u32[]{:S(2)}, u32[]{:S(2)}) collective-permute-start(bf16[2,384,512]{2,1,0:T(8,128)(2,1)} %fusion.31), channel_id=1, source_target_pairs={{4,0},{8,4},{12,8},{16,12},{20,16},{24,20},{28,24},{5,1},{9,5},{13... | collective-permute-start | bytes 2359304 | tf_op jit(solution)/shard_map/ppermute | solution.py:19
  241.0 7.7 %copy-start.28 = (f32[1,384,512]{2,1,0:T(8,128)S(1)}, f32[1,384,512]{2,1,0:T(8,128)}, u32[]{:S(2)}) copy-start(f32[1,384,512]{2,1,0:T(8,128)} %copy.451) | copy-start | bytes 2359300
  241.0 7.7 %copy-start.29 = (f32[1,384,512]{2,1,0:T(8,128)S(1)}, f32[1,384,512]{2,1,0:T(8,128)}, u32[]{:S(2)}) copy-start(f32[1,384,512]{2,1,0:T(8,128)} %copy.450) | copy-start | bytes 2359300
  289.4 290.5 %reduce-scatter.5.cloned.1.call-start = ((), (), s32[]{:S(2)}) async-start(), calls=%async_computation.3 | async-start | bytes 3686400 | tf_op jit(solution)/shard_map/reduce_scatter | solution.py:222
  (59 other events, 159.8 us)
Sparse Core Ops, SparseCore 0:
  9.6 30.1 all-gather.1
  289.6 251.3 reduce-scatter.6
  544.1 35.8 reduce-scatter.4
where the time goes:
time: 597 us; the launch traced here: 587 us
  waiting for transfers between devices  326 us (55%)
  local copies, waits for them, and re-layouts  119 us (20%)
  matrix products  79.7 us (13%)
  other arithmetic  28.8 us (5%)
  starting transfers between devices  18.4 us (3%)
  between operations  14.9 us (2%)
    unnamed x4, waiting for transfers between devices  237 us
    unnamed x165, local copies, waits for them, and re-layouts  50.1 us
    reduce_scatter x1, waiting for transfers between devices, on_device(): lax.psum_scatter(input_terms.astype(jnp.bfloat16), 'head', scatter_dimens...  35.6 us
    ppermute x6, waiting for transfers between devices, passed_along(): return lax.ppermute(block, axis, route)  29.6 us
    all_gather x1, waiting for transfers between devices, on_device(): gathered = lax.all_gather(tokens, 'head', axis=0, tiled=True)  23.9 us
    ppermute x6, starting transfers between devices, passed_along(): return lax.ppermute(block, axis, route)  18 us
    another operation x8, local copies, waits for them, and re-layouts, back_block(): jnp.stack([key_grad.reshape(row_count, groups * head_width), value_grad.r...  16.5 us
  transfers between devices with their start and end apart: 9, of which 8 were waited for; matrix products, arithmetic and copies ran while one was open for 18% of the time, Pallas kernels for 0%

commit v1 on v0

v1 whole, which is shorter than its diff:
```python
from functools import partial
import math

import jax
import jax.numpy as jnp
from jax import lax
from jax.experimental import pallas as pl
from jax.experimental.pallas import tpu as pltpu
from jax.sharding import PartitionSpec as P

WINDOW = 1024
TILE = 128

norm_eps = 1e-06
rope_base = 10000.0

NT = (((1,), (1,)), ((), ()))
NN = (((1,), (0,)), ((), ()))
TN = (((0,), (0,)), ((), ()))


def mm(a, b, dims):
    return lax.dot_general(a, b, dims, preferred_element_type=jnp.float32)


def shifted(block, axis, distance):
    count = lax.axis_size(axis)
    route = [(i, i + distance) for i in range(count) if 0 <= i + distance < count]
    return lax.ppermute(block, axis, route)


def rope_tables(positions, head_width):
    half_width = head_width // 2
    indices = jnp.arange(half_width, dtype=jnp.float32)
    frequency = jnp.power(rope_base, -2.0 * indices / head_width)
    angles = positions.astype(jnp.float32)[:, None] * frequency[None, :]
    return (jnp.cos(angles), jnp.sin(angles))


def rotate(vector, cosine_table, sine_table):
    half_width = vector.shape[-1] // 2
    lower = vector[..., :half_width]
    upper = vector[..., half_width:]
    return jnp.concatenate(
        [
            lower * cosine_table - upper * sine_table,
            upper * cosine_table + lower * sine_table,
        ],
        axis=-1,
    )


def normalize(vector, gain_vector):
    inv_rms = lax.rsqrt(jnp.mean(vector * vector, axis=-1, keepdims=True) + norm_eps)
    return (vector * inv_rms * gain_vector, inv_rms)


def norm_back(vector, inv_rms, gain_vector, upstream):
    scaled = upstream * gain_vector
    return inv_rms * scaled - vector * (inv_rms * inv_rms * inv_rms) * jnp.mean(
        vector * scaled, axis=-1, keepdims=True
    )


def attention_kernel(reach, heads, width, *refs):
    q_ref, go_ref, cos_ref, sin_ref, limit_ref, gain_ref = refs[:6]
    kv_refs = refs[6 : 7 + reach]
    att_ref, qg_ref = refs[7 + reach : 9 + reach]
    dkv_refs = refs[9 + reach : 10 + 2 * reach]
    kcat, vcat, dk_acc, dv_acc = refs[10 + 2 * reach :]
    tile = pl.program_id(1)
    span = WINDOW + TILE
    scale = 1.0 / math.sqrt(width)

    @pl.when(tile == 0)
    def _():
        row = 0
        for ref in kv_refs:
            rows = ref.shape[0]
            kcat[row : row + rows, :] = ref[:, :width]
            vcat[row : row + rows, :] = ref[:, width:]
            row += rows
        dk_acc[...] = jnp.zeros_like(dk_acc)
        dv_acc[...] = jnp.zeros_like(dv_acc)

    gain = gain_ref[...]
    cosine = cos_ref[...]
    sine = sin_ref[...]
    raws = [q_ref[:, h * width : (h + 1) * width] for h in range(heads)]
    states, invs = [], []
    for raw in raws:
        normed, inv = normalize(raw, gain)
        states.append((rotate(normed, cosine, sine) * scale).astype(jnp.bfloat16))
        invs.append(inv)
    q = jnp.concatenate(states, axis=0)
    go = jnp.concatenate(
        [go_ref[:, h * width : (h + 1) * width] for h in range(heads)], axis=0
    )
    start = pl.multiple_of(tile * TILE, TILE)
    k = kcat[pl.ds(start, span), :]
    v = vcat[pl.ds(start, span), :]
    scores = mm(q, k, NT)
    distance = (
        WINDOW
        + lax.broadcasted_iota(jnp.int32, (TILE, span), 0)
        - lax.broadcasted_iota(jnp.int32, (TILE, span), 1)
    )
    visible = (distance >= 0) & (distance <= limit_ref[...])
    bias = jnp.where(visible, 0.0, -jnp.inf)
    scores = scores + jnp.concatenate([bias] * heads, axis=0)
    peak = jnp.max(scores, axis=-1, keepdims=True)
    weights = jnp.exp(scores - peak)
    total = jnp.sum(weights, axis=-1, keepdims=True)
    probs = weights * (1.0 / total)
    probs_bf = probs.astype(jnp.bfloat16)
    attended = mm(probs_bf, v, NN).astype(jnp.bfloat16)
    for h in range(heads):
        att_ref[:, h * width : (h + 1) * width] = attended[h * TILE : (h + 1) * TILE]
    delta = jnp.sum(
        go.astype(jnp.float32) * attended.astype(jnp.float32), axis=-1, keepdims=True
    )
    dprobs = mm(go, v, NT)
    dscores = (probs * (dprobs - delta)).astype(jnp.bfloat16)
    dq = mm(dscores, k, NN)
    dk_acc[pl.ds(start, span), :] += mm(dscores, q, TN)
    dv_acc[pl.ds(start, span), :] += mm(probs_bf, go, TN)
    for h in range(heads):
        up = rotate(dq[h * TILE : (h + 1) * TILE], cosine, -sine) * scale
        qg_ref[:, h * width : (h + 1) * width] = norm_back(
            raws[h], invs[h], gain, up
        ).astype(jnp.bfloat16)

    @pl.when(tile == pl.num_programs(1) - 1)
    def _():
        row = 0
        for ref in dkv_refs:
            rows = ref.shape[0]
            ref[:, :width] = dk_acc[row : row + rows, :].astype(ref.dtype)
            ref[:, width:] = dv_acc[row : row + rows, :].astype(ref.dtype)
            row += rows


def attention(q_raw, out_grad, cosine, sine, limit, gain, kv_blocks, groups):
    row_count, columns = q_raw.shape
    width = gain.shape[-1]
    heads = columns // groups // width
    reach = len(kv_blocks) - 1
    own = pl.BlockSpec((TILE, heads * width), lambda g, t: (t, g))
    table = pl.BlockSpec((TILE, width // 2), lambda g, t: (t, 0))
    kv_specs = [
        pl.BlockSpec((block.shape[0], 2 * width), lambda g, t: (0, g)) for block in kv_blocks
    ]
    keys = WINDOW + row_count
    flops = 6 * 2 * row_count * heads * groups * (WINDOW + TILE) * width
    return pl.pallas_call(
        partial(attention_kernel, reach, heads, width),
        grid=(groups, row_count // TILE),
        in_specs=[
            own,
            own,
            table,
            table,
            pl.BlockSpec((TILE, 1), lambda g, t: (t, 0)),
            pl.BlockSpec((1, width), lambda g, t: (0, 0)),
        ]
        + kv_specs,
        out_specs=[own, own] + kv_specs,
        out_shape=[
            jax.ShapeDtypeStruct((row_count, columns), jnp.bfloat16),
            jax.ShapeDtypeStruct((row_count, columns), jnp.bfloat16),
        ]
        + [
            jax.ShapeDtypeStruct(block.shape, jnp.bfloat16 if i < reach else jnp.float32)
            for i, block in enumerate(kv_blocks)
        ],
        scratch_shapes=[
            pltpu.VMEM((keys, width), jnp.bfloat16),
            pltpu.VMEM((keys, width), jnp.bfloat16),
            pltpu.VMEM((keys, width), jnp.float32),
            pltpu.VMEM((keys, width), jnp.float32),
        ],
        compiler_params=pltpu.CompilerParams(vmem_limit_bytes=40 * 1024 * 1024),
        cost_estimate=pl.CostEstimate(
            flops=flops, bytes_accessed=16 * 1024 * 1024, transcendentals=2 * 1024 * 1024
        ),
    )(q_raw, out_grad, cosine, sine, limit, gain, *kv_blocks)


def head_sum(terms, axis):
    count = lax.axis_size(axis)
    me = lax.axis_index(axis)
    pieces = terms.reshape(count, terms.shape[0] // count, terms.shape[1])
    total = lax.dynamic_index_in_dim(pieces, me, 0, keepdims=False).astype(jnp.float32)
    for distance in range(1, count):
        piece = lax.dynamic_index_in_dim(
            pieces, lax.rem(me + distance, count), 0, keepdims=False
        )
        got = lax.ppermute(piece, axis, [(i, (i + distance) % count) for i in range(count)])
        total = total + got.astype(jnp.float32)
    return total.astype(jnp.bfloat16)


def on_device(tokens, w_query, w_key, w_value, query_gain, key_gain, positions, out_grad):
    gathered = lax.all_gather(tokens, "head", axis=0, tiled=True)
    row_count, model_width = gathered.shape
    width = query_gain.shape[0]
    groups = w_key.shape[1] // width
    rank_count = lax.axis_size("ctx")
    head_ranks = lax.axis_size("head")
    my_rank = lax.axis_index("ctx")
    reach = (WINDOW + row_count - 1) // row_count
    sub_rows = tokens.shape[0]
    out_rows = model_width // rank_count

    value_states = mm(gathered, w_value, NN).astype(jnp.bfloat16)
    key_raw = mm(gathered, w_key, NN).reshape(row_count, groups, width)
    cosine, sine = rope_tables(positions, width)
    key_normed, key_inv = normalize(key_raw, key_gain)
    key_states = rotate(key_normed, cosine[:, None, :], sine[:, None, :]).astype(jnp.bfloat16)
    value_parts = value_states.reshape(row_count, groups, width)
    local_kv = jnp.concatenate([key_states, value_parts], axis=-1).reshape(
        row_count, groups * 2 * width
    )
    skipped = [max(0, stride * row_count - WINDOW) for stride in range(reach + 1)]
    kv_blocks = [
        shifted(local_kv[skipped[stride] :], "ctx", stride) for stride in range(reach, 0, -1)
    ] + [local_kv]

    query_raw = mm(gathered, w_query, NN)
    rows = jnp.arange(row_count, dtype=jnp.int32)
    limit = jnp.minimum(jnp.minimum(positions, WINDOW - 1), my_rank * row_count + rows)[:, None]
    attended, query_raw_grad, *dkv = attention(
        query_raw, out_grad, cosine, sine, limit, query_gain[None, :], kv_blocks, groups
    )

    stripes = [list(range(first, rank_count, 2)) for first in range(2)]
    pairs = rank_count // 2
    spread = lax.all_to_all(
        tokens.reshape(sub_rows, pairs, 2 * out_rows).swapaxes(0, 1),
        "ctx",
        0,
        0,
        axis_index_groups=stripes,
    )
    columns = lax.all_gather(spread, "head", axis=1, tiled=True)
    columns = columns.reshape(pairs * row_count, 2, out_rows)
    side = lax.rem(my_rank, 2)
    own_columns = lax.dynamic_index_in_dim(columns, side, 1, keepdims=False)
    pair_columns = lax.dynamic_index_in_dim(columns, 1 - side, 1, keepdims=False)
    swap = [(i, i + 1 - 2 * (i % 2)) for i in range(rank_count)]

    def weight_grad(grads):
        sent = mm(pair_columns, grads, TN).astype(jnp.bfloat16)
        got = lax.ppermute(sent, "ctx", swap)
        return (mm(own_columns, grads, TN) + got.astype(jnp.float32)).astype(jnp.bfloat16)

    query_all = lax.all_gather(
        query_raw_grad, "ctx", axis=0, tiled=True, axis_index_groups=stripes
    )

    dkv_sum = dkv[reach]
    for stride in range(1, reach + 1):
        back = shifted(dkv[reach - stride], "ctx", -stride).astype(jnp.float32)
        dkv_sum = dkv_sum + jnp.pad(back, ((skipped[stride], 0), (0, 0)))
    dkv_parts = dkv_sum.reshape(row_count, groups, 2 * width)
    key_raw_grad = (
        norm_back(
            key_raw,
            key_inv,
            key_gain,
            rotate(dkv_parts[..., :width], cosine[:, None, :], -sine[:, None, :]),
        )
        .astype(jnp.bfloat16)
        .reshape(row_count, groups * width)
    )
    value_grads = dkv_parts[..., width:].astype(jnp.bfloat16).reshape(row_count, groups * width)
    kv_all = lax.all_gather(
        jnp.concatenate([key_raw_grad, value_grads], axis=1),
        "ctx",
        axis=0,
        tiled=True,
        axis_index_groups=stripes,
    )
    input_terms = (
        mm(query_raw_grad, w_query, NT)
        + mm(key_raw_grad, w_key, NT)
        + mm(value_grads, w_value, NT)
    )
    input_grad = head_sum(input_terms.astype(jnp.bfloat16), "head")
    grad_query = weight_grad(query_all)
    grad_kv = weight_grad(kv_all)
    key_cols = groups * width
    return (
        attended,
        input_grad,
        grad_query,
        grad_kv[:, :key_cols],
        grad_kv[:, key_cols:],
    )


def solution(mesh):
    in_specs = (
        P(("ctx", "head"), None),
        P(None, "head"),
        P(None, "head"),
        P(None, "head"),
        P(),
        P(),
        P("ctx"),
        P("ctx", "head"),
    )
    out_specs = (
        P("ctx", "head"),
        P(("ctx", "head"), None),
        P("ctx", "head"),
        P("ctx", "head"),
        P("ctx", "head"),
    )
    return jax.shard_map(
        on_device, mesh=mesh, in_specs=in_specs, out_specs=out_specs, check_vma=False
    )
```

time: 597 us -> 338 us (0.57); the launches traced: 587 us -> 338 us
  waiting for transfers between devices: 326 us -> 146 us
  local copies, waits for them, and re-layouts: 119 us -> 27.8 us
  matrix products: 79.7 us -> 47.4 us
  starting transfers between devices: 18.4 us -> 49.4 us
  blocking collectives: 0 us -> 26.2 us
  other arithmetic: 28.8 us -> 12.4 us
  Pallas kernels: 0 us -> 13.7 us
    unnamed x4, waiting for transfers between devices: 237 us -> 0.73 us
    ppermute x6 -> x11, waiting for transfers between devices: 29.6 us -> 122 us  [the longest x6 107 us: shifted(): return lax.ppermute(block, axis, route)]
    unnamed x165 -> x51, local copies, waits for them, and re-layouts: 50.1 us -> 4.23 us
    another operation x19 -> x0, local copies, waits for them, and re-layouts: 36.9 us -> none  [the longest x8 16.5 us: back_block(): jnp.stack([key_grad.reshape(row_count, groups * head_width), value_grad.r...]
    reduce_scatter x1 -> x0, waiting for transfers between devices: 35.6 us -> none  [on_device(): lax.psum_scatter(input_terms.astype(jnp.bfloat16), 'head', scatter_dimens...]
    dot_general x31 -> x10, matrix products: 79.7 us -> 47.4 us  [mm(): return lax.dot_general(a, b, dims, preferred_element_type=jnp.float32)]
    ppermute x6 -> x11, starting transfers between devices: 18 us -> 49.2 us  [the longest x2 34.2 us: weight_grad(): got = lax.ppermute(sent, 'ctx', swap)]
    all_to_all x0 -> x1, blocking collectives: none -> 26.2 us  [on_device(): lax.all_to_all(tokens.reshape(sub_rows, pairs, 2 * out_rows).swapaxes(0,...]
  transfers between devices with their start and end apart: 9 -> 15, of which waited for: 8 -> 4; matrix products, arithmetic and copies ran while one was open for 18% -> 25% of each run, Pallas kernels for 0% -> 4%
where the time goes in v1:
time: 338 us
  waiting for transfers between devices  146 us (43%)
  starting transfers between devices  49.4 us (15%)
  matrix products  47.4 us (14%)
  local copies, waits for them, and re-layouts  27.8 us (8%)
  blocking collectives  26.2 us (8%)
  between operations  14.3 us (4%)
  Pallas kernels  13.7 us (4%)
  other arithmetic  12.4 us (4%)
    ppermute x6, waiting for transfers between devices, shifted(): return lax.ppermute(block, axis, route)  107 us
    dot_general x10, matrix products, mm(): return lax.dot_general(a, b, dims, preferred_element_type=jnp.float32)  47.4 us
    ppermute x2, starting transfers between devices, weight_grad(): got = lax.ppermute(sent, 'ctx', swap)  34.2 us
    all_to_all x1, blocking collectives, on_device(): lax.all_to_all(tokens.reshape(sub_rows, pairs, 2 * out_rows).swapaxes(0,...  26.2 us
    all_gather x1, waiting for transfers between devices, on_device(): lax.all_gather(jnp.concatenate([key_raw_grad, value_grads], axis=1), 'ctx...  23.4 us
    ppermute x2, waiting for transfers between devices, weight_grad(): got = lax.ppermute(sent, 'ctx', swap)  14.9 us
    ppermute x6, starting transfers between devices, shifted(): return lax.ppermute(block, axis, route)  14.5 us
    pallas_call x1, Pallas kernels, attention(): pl.pallas_call(partial(attention_kernel, reach, heads, width), grid=(grou...  13.7 us
  transfers between devices with their start and end apart: 15, of which 4 were waited for; matrix products, arithmetic and copies ran while one was open for 25% of the time, Pallas kernels for 4%

profile of v1, /device:TPU:0, one launch (start us, length us, event | category | flops | bytes accessed | tf_op | source)
XLA Modules:
  0.0 337.7 jit_solution(13882893762008512224)
XLA Ops:
  10.9 26.2 %all_to_all.5 = bf16[4,96,960]{2,1,0:T(8,128)(2,1)S(1)} all-to-all(bf16[4,96,960]{2,1,0:T(8,128)(2,1)S(1)} %copy.35), channel_id=1, replica_groups={{0,8,16,24},{4,12,20,28},{1,9,17,25},{5,13,21,29},{2,10,18,26},{6,14,22..., dimensions={0} | all-to-all | bytes 1474560 | tf_op jit(solution)/shard_map/all_to_all | solution.py:238
  40.3 4.7 %convolution_convert_fusion = bf16[384,512]{1,0:T(8,128)(2,1)S(1)} fusion(bf16[384,3840]{1,0:T(8,128)(2,1)} %all-gather.5.cloned.1.call-done, bf16[3840,512]{1,0:T(8,128)(2,1)} %param.11), kind=kOutput, calls=%fused_computation.21 | convolution fusion | flops 1510146048 | bytes 7274496 | tf_op jit(solution)/shard_map/dot_general | solution.py:23
  45.1 5.0 %fusion.29 = f32[384,512]{1,0:T(8,128)S(1)} fusion(bf16[384,3840]{1,0:T(8,128)(2,1)} %all-gather.5.cloned.1.call-done, bf16[3840,512]{1,0:T(8,128)(2,1)} %param.10), kind=kOutput, calls=%fused_computation.52 | convolution fusion | flops 1509949440 | bytes 7667712 | tf_op jit(solution)/shard_map/dot_general | solution.py:23
  56.2 3.4 %collective-permute-start.2 = (bf16[384,1024]{1,0:T(8,128)(2,1)S(1)}, bf16[384,1024]{1,0:T(8,128)(2,1)S(1)}, u32[]{:S(2)}, u32[]{:S(2)}) collective-permute-start(bf16[384,1024]{1,0:T(8,128)(2,1)S(1)} %bitcast.64), channel_id=1, source_target_pairs={{0,4},{4,8},{8,12},{12,16},{16,20},{20,24},{24,28},{1,5},{5,9},{9,... | collective-permute-start | bytes 2359304 | tf_op jit(solution)/shard_map/ppermute | solution.py:29
  59.8 4.6 %collective-permute-start = (bf16[256,1024]{1,0:T(8,128)(2,1)S(1)}, bf16[256,1024]{1,0:T(8,128)(2,1)S(1)}, u32[]{:S(2)}, u32[]{:S(2)}) collective-permute-start(bf16[256,1024]{1,0:T(8,128)(2,1)S(1)} %bitcast.83), channel_id=1, source_target_pairs={{0,12},{4,16},{8,20},{12,24},{16,28},{1,13},{5,17},{9,21},{13,25},... | collective-permute-start | bytes 1572872 | tf_op jit(solution)/shard_map/ppermute | solution.py:29
  64.3 5.5 %fusion.28.refs_0_ = f32[384,1024]{1,0:T(8,128)S(1)} fusion(bf16[384,3840]{1,0:T(8,128)(2,1)S(1)} %copy-done.20, bf16[3840,1024]{1,0:T(8,128)(2,1)} %param.9), kind=kOutput, calls=%fused_computation.51 | convolution fusion | flops 3019898880 | bytes 12386304 | tf_op jit(solution)/shard_map/dot_general | solution.py:23
  69.9 14.8 %collective-permute-done.refs_6_ = bf16[256,1024]{1,0:T(8,128)(2,1)S(1)} collective-permute-done((bf16[256,1024]{1,0:T(8,128)(2,1)S(1)}, bf16[256,1024]{1,0:T(8,128)(2,1)S(1)}, u32[]{:S(2)}, u32[]{:S(2)}) %collective-permute-start) | collective-permute-done | bytes 524320 | tf_op jit(solution)/shard_map/ppermute | solution.py:29
  84.7 13.7 %shard_map.119 = (bf16[384,1024]{1,0:T(8,128)(2,1)}, bf16[384,1024]{1,0:T(8,128)(2,1)}, bf16[256,1024]{1,0:T(8,128)(2,1)S(1)}, bf16[384,1024]{1,0:T(8,128)(2,1)S...) custom-call(f32[384,1024]{1,0:T(8,128)S(1)} %fusion.28.refs_0_, bf16[384,1024]{1,0:T(8,128)(2,1)S(1)} %copy-done, ...), custom_call_target="tpu_custom_call" | custom-call | flops 5435817984 | bytes 16777216 | tf_op jit(solution)/shard_map/pallas_call | solution.py:155
  106.5 92.5 %collective-permute-done.5 = bf16[256,1024]{1,0:T(8,128)(2,1)} collective-permute-done((bf16[256,1024]{1,0:T(8,128)(2,1)S(1)}, bf16[256,1024]{1,0:T(8,128)(2,1)}, u32[]{:S(2)}, u32[]{:S(2)}) %collective-permute-start.5) | collective-permute-done | bytes 524320 | tf_op jit(solution)/shard_map/ppermute | solution.py:29
  198.9 3.1 convert_add_fusion
  202.1 2.7 reshape.136
  209.5 6.0 %copy.37 = bf16[4,384,960]{1,0,2:T(4,128)(2,1)S(1)} copy(bf16[4,384,960]{2,0,1:T(4,128)(2,1)} %all-gather.7.cloned.1.call-done) | data formatting | bytes 5898240 | tf_op jit(solution)/shard_map/all_gather | solution.py:245
  215.5 3.2 reshape.140
  218.7 4.0 %fusion.31 = f32[384,3840]{1,0:T(8,128)S(1)} fusion(bf16[384,512]{1,0:T(8,128)(2,1)S(1)} %bitcast.69, bf16[3840,512]{1,0:T(8,128)(2,1)} %param.11), kind=kOutput, calls=%fused_computation.54 | convolution fusion | flops 1509949440 | bytes 10223616 | tf_op jit(solution)/shard_map/dot_general | solution.py:23
  222.7 4.3 %fusion.30 = f32[384,3840]{1,0:T(8,128)} fusion(bf16[384,512]{1,0:T(8,128)(2,1)S(1)} %copy-done.7, bf16[3840,512]{1,0:T(8,128)(2,1)S(1)} %copy-done.5), kind=kOutput, calls=%fused_computation.53 | convolution fusion | flops 1509949440 | bytes 10223616 | tf_op jit(solution)/shard_map/dot_general | solution.py:23
  227.0 10.1 %add_convert_fusion = bf16[384,3840]{1,0:T(8,128)(2,1)} fusion(f32[384,3840]{1,0:T(8,128)S(1)} %fusion.31, f32[384,3840]{1,0:T(8,128)} %fusion.30, bf16[384,1024]{1,0:T(8,128)(2,1)} %get-tuple-element.12, bf16[3840,1024]{1,0:T(8,128)(2,1)} %param.9), kind=kOutput, calls=%fused_computation | convolution fusion | flops 3024322560 | bytes 23396352 | tf_op jit(solution)/shard_map/dot_general | solution.py:23
  237.2 3.1 dynamic-slice_bitcast_fusion.2
  240.8 4.5 %fusion.10 = bf16[480,1024]{1,0:T(8,128)(2,1)} fusion(bf16[1536,1024]{1,0:T(8,128)(2,1)} %all-gather.9.cloned.1.call-done, bf16[1536,2,480]{0,2,1:T(8,128)(2,1)S(1)} %copy-done.12, s32[]{:T(128)S(6)} %select_n.25), kind=kOutput, calls=%fused_computation.15 | convolution fusion | flops 1510440960 | bytes 5603332 | tf_op jit(solution)/shard_map/dot_general | solution.py:23
  245.3 32.6 %collective-permute-start.9 = (bf16[480,1024]{1,0:T(8,128)(2,1)}, bf16[480,1024]{1,0:T(8,128)(2,1)}, u32[]{:S(2)}, u32[]{:S(2)}) collective-permute-start(bf16[480,1024]{1,0:T(8,128)(2,1)} %fusion.10), channel_id=1, source_target_pairs={{0,4},{4,0},{8,12},{12,8},{16,20},{20,16},{24,28},{28,24},{1,5},{5... | collective-permute-start | bytes 2949128 | tf_op jit(solution)/shard_map/ppermute | solution.py:254
  278.0 23.4 %all-gather.11.cloned.1.call-done = bf16[1536,1024]{1,0:T(8,128)(2,1)} async-done(((bf16[384,1024]{1,0:T(8,128)(2,1)}), bf16[1536,1024]{1,0:T(8,128)(2,1)}) %all-gather.11.cloned.1.call-update) | async-done | bytes 3145744 | tf_op jit(solution)/shard_map/all_gather | solution.py:277
  301.4 3.6 %fusion.13 = bf16[480,1024]{1,0:T(8,128)(2,1)S(1)} fusion(bf16[1536,1024]{1,0:T(8,128)(2,1)} %all-gather.11.cloned.1.call-done, bf16[1536,2,480]{0,2,1:T(8,128)(2,1)S(1)} %copy-done.12, s32[]{:T(128)S(6)} %select_n.25), kind=kOutput, calls=%fused_computation.16 | convolution fusion | flops 1510440960 | bytes 5603332 | tf_op jit(solution)/shard_map/dot_general | solution.py:23
  306.5 3.0 fusion.2
  309.5 4.0 %add_convert_fusion.2 = bf16[480,1024]{1,0:T(8,128)(2,1)} fusion(bf16[480,1024]{1,0:T(8,128)(2,1)} %collective-permute-done.9, bf16[1536,1024]{1,0:T(8,128)(2,1)S(1)} %copy-done.18, bf16[1536,2,480]{0,2,1:T(8,128)(2,1)S(1)} %copy-done.12, s32[]{:T(128)S(6)} %select_n.24), kind=kOutput, calls=%fused_computation.2 | convolution fusion | flops 1511424000 | bytes 6586372 | tf_op jit(solution)/shard_map/dot_general | solution.py:23
  313.5 14.9 %collective-permute-done.10 = bf16[480,1024]{1,0:T(8,128)(2,1)S(1)} collective-permute-done((bf16[480,1024]{1,0:T(8,128)(2,1)S(1)}, bf16[480,1024]{1,0:T(8,128)(2,1)S(1)}, u32[]{:S(2)}, u32[]{:S(2)}) %collective-permute-start.10) | collective-permute-done | bytes 983072 | tf_op jit(solution)/shard_map/ppermute | solution.py:254
  (107 shorter events, 30.4 us)
Async XLA Ops:
  7.2 33.2 %all-gather.5.cloned.1.call-start = ((), (), s32[]{:S(2)}) async-start(), calls=%async_computation.1 | async-start | bytes 3686400 | tf_op jit(solution)/shard_map/all_gather | solution.py:204
  7.9 201.6 %all-gather.7.cloned.1.call-start = ((), (), s32[]{:S(2)}) async-start(), calls=%async_computation.2 | async-start | bytes 3932160 | tf_op jit(solution)/shard_map/all_gather | solution.py:245
  10.6 28.1 %copy-start.17 = (s32[384]{0:T(512)S(1)}, s32[384]{0:T(512)}, u32[]{:S(2)}) copy-start(s32[384]{0:T(512)} %param.14) | copy-start | bytes 4612
  38.7 202.1 %all-gather.9.cloned.1.call-start = ((), (), s32[]{:S(2)}) async-start(), calls=%async_computation.3 | async-start | bytes 3932160 | tf_op jit(solution)/shard_map/all_gather | solution.py:257
  52.4 12.0 %copy-start.20 = (bf16[384,3840]{1,0:T(8,128)(2,1)S(1)}, bf16[384,3840]{1,0:T(8,128)(2,1)}, u32[]{:S(2)}) copy-start(bf16[384,3840]{1,0:T(8,128)(2,1)} %all-gather.5.cloned.1.call-done) | copy-start | bytes 8847364
  53.7 31.0 %collective-permute-start.1 = (bf16[384,1024]{1,0:T(8,128)(2,1)S(1)}, bf16[384,1024]{1,0:T(8,128)(2,1)S(1)}, u32[]{:S(2)}, u32[]{:S(2)}) collective-permute-start(bf16[384,1024]{1,0:T(8,128)(2,1)S(1)} %bitcast.63), channel_id=1, source_target_pairs={{0,8},{4,12},{8,16},{12,20},{16,24},{20,28},{1,9},{5,13},{9,17},{1... | collective-permute-start | bytes 2359304 | tf_op jit(solution)/shard_map/ppermute | solution.py:29
  56.2 28.4 %collective-permute-start.2 = (bf16[384,1024]{1,0:T(8,128)(2,1)S(1)}, bf16[384,1024]{1,0:T(8,128)(2,1)S(1)}, u32[]{:S(2)}, u32[]{:S(2)}) collective-permute-start(bf16[384,1024]{1,0:T(8,128)(2,1)S(1)} %bitcast.64), channel_id=1, source_target_pairs={{0,4},{4,8},{8,12},{12,16},{16,20},{20,24},{24,28},{1,5},{5,9},{9,... | collective-permute-start | bytes 2359304 | tf_op jit(solution)/shard_map/ppermute | solution.py:29
  59.7 24.9 %copy-start = (bf16[384,1024]{1,0:T(8,128)(2,1)S(1)}, bf16[384,1024]{1,0:T(8,128)(2,1)}, u32[]{:S(2)}) copy-start(bf16[384,1024]{1,0:T(8,128)(2,1)} %refs_1_.1) | copy-start | bytes 2359300
  59.7 24.9 %copy-start.2 = (f32[256]{0:T(256)S(1)}, f32[256]{0:T(256)}, u32[]{:S(2)}) copy-start(f32[256]{0:T(256)} %param.12) | copy-start | bytes 3076
  59.8 24.9 %collective-permute-start = (bf16[256,1024]{1,0:T(8,128)(2,1)S(1)}, bf16[256,1024]{1,0:T(8,128)(2,1)S(1)}, u32[]{:S(2)}, u32[]{:S(2)}) collective-permute-start(bf16[256,1024]{1,0:T(8,128)(2,1)S(1)} %bitcast.83), channel_id=1, source_target_pairs={{0,12},{4,16},{8,20},{12,24},{16,28},{1,13},{5,17},{9,21},{13,25},... | collective-permute-start | bytes 1572872 | tf_op jit(solution)/shard_map/ppermute | solution.py:29
  99.3 5.7 %copy-start.14 = (f32[384,2]{1,0:T(8,128)S(1)}, f32[384,2]{1,0:T(8,128)}, u32[]{:S(2)}) copy-start(f32[384,2]{1,0:T(8,128)} %copy-done.13) | copy-start | bytes 9220
  99.3 202.0 %all-gather.11.cloned.1.call-start = ((), (), s32[]{:S(2)}) async-start(), calls=%async_computation.4 | async-start | bytes 3932160 | tf_op jit(solution)/shard_map/all_gather | solution.py:277
  99.4 99.5 %collective-permute-start.4 = (bf16[384,1024]{1,0:T(8,128)(2,1)}, bf16[384,1024]{1,0:T(8,128)(2,1)}, u32[]{:S(2)}, u32[]{:S(2)}) collective-permute-start(bf16[384,1024]{1,0:T(8,128)(2,1)} %copy-done.1), channel_id=1, source_target_pairs={{8,0},{12,4},{16,8},{20,12},{24,16},{28,20},{9,1},{13,5},{17,9},{2... | collective-permute-start | bytes 2359304 | tf_op jit(solution)/shard_map/ppermute | solution.py:29
  100.8 98.1 %collective-permute-start.3 = (bf16[384,1024]{1,0:T(8,128)(2,1)S(1)}, bf16[384,1024]{1,0:T(8,128)(2,1)}, u32[]{:S(2)}, u32[]{:S(2)}) collective-permute-start(bf16[384,1024]{1,0:T(8,128)(2,1)S(1)} %get-tuple-element.14), channel_id=1, source_target_pairs={{4,0},{8,4},{12,8},{16,12},{20,16},{24,20},{28,24},{5,1},{9,5},{13... | collective-permute-start | bytes 2359304 | tf_op jit(solution)/shard_map/ppermute | solution.py:29
  102.1 96.8 %collective-permute-start.5 = (bf16[256,1024]{1,0:T(8,128)(2,1)S(1)}, bf16[256,1024]{1,0:T(8,128)(2,1)}, u32[]{:S(2)}, u32[]{:S(2)}) collective-permute-start(bf16[256,1024]{1,0:T(8,128)(2,1)S(1)} %get-tuple-element.16), channel_id=1, source_target_pairs={{12,0},{16,4},{20,8},{24,12},{28,16},{13,1},{17,5},{21,9},{25,13},... | collective-permute-start | bytes 1572872 | tf_op jit(solution)/shard_map/ppermute | solution.py:29
  218.7 4.0 %copy-start.5 = (bf16[3840,512]{1,0:T(8,128)(2,1)S(1)}, bf16[3840,512]{1,0:T(8,128)(2,1)}, u32[]{:S(2)}) copy-start(bf16[3840,512]{1,0:T(8,128)(2,1)} %param.10) | copy-start | bytes 11796484
  218.7 4.0 %copy-start.7 = (bf16[384,512]{1,0:T(8,128)(2,1)S(1)}, bf16[384,512]{1,0:T(8,128)(2,1)}, u32[]{:S(2)}) copy-start(bf16[384,512]{1,0:T(8,128)(2,1)} %copy-done.6) | copy-start | bytes 1179652
  240.3 66.2 %collective-permute-start.8 = (bf16[96,3840]{1,0:T(8,128)(2,1)}, bf16[96,3840]{1,0:T(8,128)(2,1)}, u32[]{:S(2)}, u32[]{:S(2)}) collective-permute-start(bf16[96,3840]{1,0:T(8,128)(2,1)} %get-tuple-element.18), channel_id=1, source_target_pairs={{0,3},{1,0},{2,1},{3,2},{4,7},{5,4},{6,5},{7,6},{8,11},{9,8},{10,9... | collective-permute-start | bytes 2211848 | tf_op jit(solution)/shard_map/ppermute | solution.py:198
  240.3 66.2 %collective-permute-start.7 = (bf16[96,3840]{1,0:T(8,128)(2,1)}, bf16[96,3840]{1,0:T(8,128)(2,1)}, u32[]{:S(2)}, u32[]{:S(2)}) collective-permute-start(bf16[96,3840]{1,0:T(8,128)(2,1)} %get-tuple-element.19), channel_id=1, source_target_pairs={{0,2},{1,3},{2,0},{3,1},{4,6},{5,7},{6,4},{7,5},{8,10},{9,11},{10,... | collective-permute-start | bytes 2211848 | tf_op jit(solution)/shard_map/ppermute | solution.py:198
  240.3 66.2 %collective-permute-start.6 = (bf16[96,3840]{1,0:T(8,128)(2,1)}, bf16[96,3840]{1,0:T(8,128)(2,1)}, u32[]{:S(2)}, u32[]{:S(2)}) collective-permute-start(bf16[96,3840]{1,0:T(8,128)(2,1)} %get-tuple-element.17), channel_id=1, source_target_pairs={{0,1},{1,2},{2,3},{3,0},{4,5},{5,6},{6,7},{7,4},{8,9},{9,10},{10,1... | collective-permute-start | bytes 2211848 | tf_op jit(solution)/shard_map/ppermute | solution.py:198
  245.3 64.2 %collective-permute-start.9 = (bf16[480,1024]{1,0:T(8,128)(2,1)}, bf16[480,1024]{1,0:T(8,128)(2,1)}, u32[]{:S(2)}, u32[]{:S(2)}) collective-permute-start(bf16[480,1024]{1,0:T(8,128)(2,1)} %fusion.10), channel_id=1, source_target_pairs={{0,4},{4,0},{8,12},{12,8},{16,20},{20,16},{24,28},{28,24},{1,5},{5... | collective-permute-start | bytes 2949128 | tf_op jit(solution)/shard_map/ppermute | solution.py:254
  304.9 4.6 %copy-start.18 = (bf16[1536,1024]{1,0:T(8,128)(2,1)S(1)}, bf16[1536,1024]{1,0:T(8,128)(2,1)}, u32[]{:S(2)}) copy-start(bf16[1536,1024]{1,0:T(8,128)(2,1)} %all-gather.9.cloned.1.call-done) | copy-start | bytes 9437188
  304.9 23.5 %collective-permute-start.10 = (bf16[480,1024]{1,0:T(8,128)(2,1)S(1)}, bf16[480,1024]{1,0:T(8,128)(2,1)S(1)}, u32[]{:S(2)}, u32[]{:S(2)}) collective-permute-start(bf16[480,1024]{1,0:T(8,128)(2,1)S(1)} %fusion.13), channel_id=1, source_target_pairs={{0,4},{4,0},{8,12},{12,8},{16,20},{20,16},{24,28},{28,24},{1,5},{5... | collective-permute-start | bytes 2949128 | tf_op jit(solution)/shard_map/ppermute | solution.py:254
  309.5 19.0 %copy-start.19 = (bf16[1536,1024]{1,0:T(8,128)(2,1)S(1)}, bf16[1536,1024]{1,0:T(8,128)(2,1)}, u32[]{:S(2)}) copy-start(bf16[1536,1024]{1,0:T(8,128)(2,1)} %all-gather.11.cloned.1.call-done) | copy-start | bytes 9437188
  (12 other events, 24.3 us)
Sparse Core Ops, SparseCore 0:
  9.6 30.1 all-gather.4
  41.3 28.5 all-gather.6
  99.5 129.3 all-gather.8
  230.3 71.0 all-gather.10

commit v2 on v1

--- a/solution.py
+++ b/solution.py
@@ -249,10 +249,18 @@
     pair_columns = lax.dynamic_index_in_dim(columns, 1 - side, 1, keepdims=False)
     swap = [(i, i + 1 - 2 * (i % 2)) for i in range(rank_count)]
 
-    def weight_grad(grads):
-        sent = mm(pair_columns, grads, TN).astype(jnp.bfloat16)
+    def weight_grad(grads, own, pair):
+        sent = mm(pair, grads, TN).astype(jnp.bfloat16)
         got = lax.ppermute(sent, "ctx", swap)
-        return (mm(own_columns, grads, TN) + got.astype(jnp.float32)).astype(jnp.bfloat16)
+        return (mm(own, grads, TN) + got.astype(jnp.float32)).astype(jnp.bfloat16)
+
+    def around(stripe_columns):
+        edge = (pairs - 1) * row_count
+        padded = jnp.pad(stripe_columns, ((edge, edge), (0, 0)))
+        first = lax.div(my_rank, 2) * row_count
+        return lax.dynamic_slice_in_dim(padded, first, edge + pairs * row_count, 0)
+
+    own_around, pair_around = around(own_columns), around(pair_columns)
 
     query_all = lax.all_gather(
         query_raw_grad, "ctx", axis=0, tiled=True, axis_index_groups=stripes
@@ -274,21 +282,20 @@
         .reshape(row_count, groups * width)
     )
     value_grads = dkv_parts[..., width:].astype(jnp.bfloat16).reshape(row_count, groups * width)
-    kv_all = lax.all_gather(
-        jnp.concatenate([key_raw_grad, value_grads], axis=1),
-        "ctx",
-        axis=0,
-        tiled=True,
-        axis_index_groups=stripes,
-    )
+    upward = downward = jnp.concatenate([key_raw_grad, value_grads], axis=1)
+    kv_parts = [upward]
+    for step in range(1, pairs):
+        upward, downward = shifted(upward, "ctx", 2), shifted(downward, "ctx", -2)
+        kv_parts = [upward] + kv_parts + [downward]
+    kv_all = jnp.concatenate(kv_parts, axis=0)
     input_terms = (
         mm(query_raw_grad, w_query, NT)
         + mm(key_raw_grad, w_key, NT)
         + mm(value_grads, w_value, NT)
     )
     input_grad = head_sum(input_terms.astype(jnp.bfloat16), "head")
-    grad_query = weight_grad(query_all)
-    grad_kv = weight_grad(kv_all)
+    grad_query = weight_grad(query_all, own_columns, pair_columns)
+    grad_kv = weight_grad(kv_all, own_around, pair_around)
     key_cols = groups * width
     return (
         attended,

time: 338 us -> 378 us (1.12)
  starting transfers between devices: 49.4 us -> 103 us
  blocking collectives: 26.2 us -> 0 us
  waiting for transfers between devices: 146 us -> 154 us
  local copies, waits for them, and re-layouts: 27.8 us -> 35.3 us
    ppermute x6 -> x12, starting transfers between devices: 14.5 us -> 93.6 us  [shifted(): return lax.ppermute(block, axis, route)]
    ppermute x2, starting transfers between devices: 34.2 us -> 0.07 us  [weight_grad(): got = lax.ppermute(sent, 'ctx', swap)]
    all_to_all x1 -> x0, blocking collectives: 26.2 us -> none  [on_device(): lax.all_to_all(tokens.reshape(sub_rows, pairs, 2 * out_rows).swapaxes(0,...]
    all_gather x1 -> x0, waiting for transfers between devices: 23.4 us -> none  [on_device(): lax.all_gather(jnp.concatenate([key_raw_grad, value_grads], axis=1), 'ctx...]
    all_to_all x0 -> x1, waiting for transfers between devices: none -> 18.5 us  [on_device(): lax.all_to_all(tokens.reshape(sub_rows, pairs, 2 * out_rows).swapaxes(0,...]
    ppermute x2, waiting for transfers between devices: 14.9 us -> 26.5 us  [weight_grad(): got = lax.ppermute(sent, 'ctx', swap)]
    all_to_all x0 -> x1, starting transfers between devices: none -> 6.32 us  [on_device(): lax.all_to_all(tokens.reshape(sub_rows, pairs, 2 * out_rows).swapaxes(0,...]
    ppermute x3, waiting for transfers between devices: 0.01 us -> 5.79 us  [head_sum(): lax.ppermute(piece, axis, [(i, (i + distance) % count) for i in range(cou...]
  transfers between devices with their start and end apart: 15 -> 21, of which waited for: 4 -> 9; matrix products, arithmetic and copies ran while one was open for 25% -> 23% of each run, Pallas kernels for 4% -> 4%
where the time goes in v2:
time: 378 us; the launch traced here: 377 us
  waiting for transfers between devices  154 us (41%)
  starting transfers between devices  103 us (27%)
  matrix products  45.2 us (12%)
  local copies, waits for them, and re-layouts  35.3 us (9%)
  between operations  14.4 us (4%)
  Pallas kernels  13.9 us (4%)
  other arithmetic  10.8 us (3%)
    ppermute x12, waiting for transfers between devices, shifted(): return lax.ppermute(block, axis, route)  103 us
    ppermute x12, starting transfers between devices, shifted(): return lax.ppermute(block, axis, route)  93.6 us
    dot_general x10, matrix products, mm(): return lax.dot_general(a, b, dims, preferred_element_type=jnp.float32)  45.2 us
    ppermute x2, waiting for transfers between devices, weight_grad(): got = lax.ppermute(sent, 'ctx', swap)  26.5 us
    all_to_all x1, waiting for transfers between devices, on_device(): lax.all_to_all(tokens.reshape(sub_rows, pairs, 2 * out_rows).swapaxes(0,...  18.5 us
    pallas_call x1, Pallas kernels, attention(): pl.pallas_call(partial(attention_kernel, reach, heads, width), grid=(grou...  13.9 us
    unnamed x60, local copies, waits for them, and re-layouts  9.98 us
  transfers between devices with their start and end apart: 21, of which 9 were waited for; matrix products, arithmetic and copies ran while one was open for 23% of the time, Pallas kernels for 4%

profile of v2, /device:TPU:0, one launch (start us, length us, event | category | flops | bytes accessed | tf_op | source)
XLA Modules:
  0.0 376.7 jit_solution(2445322118635587440)
XLA Ops:
  11.7 6.3 %all-to-all-start = ((bf16[4,96,960]{2,1,0:T(8,128)(2,1)}), bf16[4,96,960]{2,1,0:T(8,128)(2,1)S(1)}, u32[]{:S(2)}, u32[]{:S(2)}) async-start(bf16[4,96,960]{2,1,0:T(8,128)(2,1)} %copy.35), calls=%async_computation | async-start | bytes 1572864 | tf_op jit(solution)/shard_map/all_to_all | solution.py:238
  19.6 18.5 %all-to-all-done = bf16[4,96,960]{2,1,0:T(8,128)(2,1)S(1)} async-done(((bf16[4,96,960]{2,1,0:T(8,128)(2,1)}), bf16[4,96,960]{2,1,0:T(8,128)(2,1)S(1)}, u32[]{:S(2)}, u32[]{:S(2)}) %all-to-all-start) | async-done | bytes 737312 | tf_op jit(solution)/shard_map/all_to_all | solution.py:238
  39.7 4.7 %fusion.13 = f32[384,512]{1,0:T(8,128)S(1)} fusion(bf16[384,3840]{1,0:T(8,128)(2,1)} %all-gather.4.cloned.1.call-done, bf16[3840,512]{1,0:T(8,128)(2,1)} %param.10), kind=kOutput, calls=%fused_computation.54 | convolution fusion | flops 1509949440 | bytes 7667712 | tf_op jit(solution)/shard_map/dot_general | solution.py:23
  45.7 5.2 %convolution_convert_fusion.1 = bf16[384,512]{1,0:T(8,128)(2,1)S(1)} fusion(bf16[384,3840]{1,0:T(8,128)(2,1)} %all-gather.4.cloned.1.call-done, bf16[3840,512]{1,0:T(8,128)(2,1)} %param.11), kind=kOutput, calls=%fused_computation.16 | convolution fusion | flops 1510146048 | bytes 7274496 | tf_op jit(solution)/shard_map/dot_general | solution.py:23
  60.2 4.6 %collective-permute-start = (bf16[256,1024]{1,0:T(8,128)(2,1)S(1)}, bf16[256,1024]{1,0:T(8,128)(2,1)S(1)}, u32[]{:S(2)}, u32[]{:S(2)}) collective-permute-start(bf16[256,1024]{1,0:T(8,128)(2,1)S(1)} %bitcast.74), channel_id=1, source_target_pairs={{0,12},{4,16},{8,20},{12,24},{16,28},{1,13},{5,17},{9,21},{13,25},... | collective-permute-start | bytes 1572872 | tf_op jit(solution)/shard_map/ppermute | solution.py:29
  64.7 5.5 %fusion.12.refs_0_ = f32[384,1024]{1,0:T(8,128)S(1)} fusion(bf16[384,3840]{1,0:T(8,128)(2,1)S(1)} %copy-done.22, bf16[3840,1024]{1,0:T(8,128)(2,1)} %param.9), kind=kOutput, calls=%fused_computation.53 | convolution fusion | flops 3019898880 | bytes 12386304 | tf_op jit(solution)/shard_map/dot_general | solution.py:23
  70.3 14.4 %collective-permute-done.refs_6_ = bf16[256,1024]{1,0:T(8,128)(2,1)S(1)} collective-permute-done((bf16[256,1024]{1,0:T(8,128)(2,1)S(1)}, bf16[256,1024]{1,0:T(8,128)(2,1)S(1)}, u32[]{:S(2)}, u32[]{:S(2)}) %collective-permute-start) | collective-permute-done | bytes 524320 | tf_op jit(solution)/shard_map/ppermute | solution.py:29
  84.7 13.9 %shard_map.119 = (bf16[384,1024]{1,0:T(8,128)(2,1)}, bf16[384,1024]{1,0:T(8,128)(2,1)}, bf16[256,1024]{1,0:T(8,128)(2,1)S(1)}, bf16[384,1024]{1,0:T(8,128)(2,1)S...) custom-call(f32[384,1024]{1,0:T(8,128)S(1)} %fusion.12.refs_0_, bf16[384,1024]{1,0:T(8,128)(2,1)S(1)} %copy-done, ...), custom_call_target="tpu_custom_call" | custom-call | flops 5435817984 | bytes 16777216 | tf_op jit(solution)/shard_map/pallas_call | solution.py:155
  105.6 55.8 %collective-permute-done.5 = bf16[256,1024]{1,0:T(8,128)(2,1)} collective-permute-done((bf16[256,1024]{1,0:T(8,128)(2,1)S(1)}, bf16[256,1024]{1,0:T(8,128)(2,1)}, u32[]{:S(2)}, u32[]{:S(2)}) %collective-permute-start.5) | collective-permute-done | bytes 524320 | tf_op jit(solution)/shard_map/ppermute | solution.py:29
  172.5 11.3 %collective-permute-start.10 = (bf16[384,1024]{1,0:T(8,128)(2,1)}, bf16[384,1024]{1,0:T(8,128)(2,1)}, u32[]{:S(2)}, u32[]{:S(2)}) collective-permute-start(bf16[384,1024]{1,0:T(8,128)(2,1)} %pad_maximum_fusion.2), channel_id=1, source_target_pairs={{0,8},{4,12},{8,16},{12,20},{16,24},{20,28},{1,9},{5,13},{9,17},{1... | collective-permute-start | bytes 2359304 | tf_op jit(solution)/shard_map/ppermute | solution.py:29
  183.8 7.1 %copy.37 = bf16[4,384,960]{1,0,2:T(4,128)(2,1)} copy(bf16[4,384,960]{2,0,1:T(4,128)(2,1)} %all-gather.6.cloned.1.call-done) | data formatting | bytes 5898240 | tf_op jit(solution)/shard_map/all_gather | solution.py:245
  190.9 4.6 %reshape.140 = bf16[1536,2,480]{0,2,1:T(8,128)(2,1)S(1)} reshape(bf16[4,384,960]{1,0,2:T(4,128)(2,1)} %copy.37) | data formatting | bytes 5898240 | tf_op jit(solution)/shard_map/reshape | solution.py:246
  198.3 50.9 %collective-permute-start.11 = (bf16[384,1024]{1,0:T(8,128)(2,1)}, bf16[384,1024]{1,0:T(8,128)(2,1)}, u32[]{:S(2)}, u32[]{:S(2)}) collective-permute-start(bf16[384,1024]{1,0:T(8,128)(2,1)} %collective-permute-done.10), channel_id=1, source_target_pairs={{0,8},{4,12},{8,16},{12,20},{16,24},{20,28},{1,9},{5,13},{9,17},{1... | collective-permute-start | bytes 2359304 | tf_op jit(solution)/shard_map/ppermute | solution.py:29
  251.0 4.2 %fusion.15 = f32[384,3840]{1,0:T(8,128)} fusion(bf16[384,512]{1,0:T(8,128)(2,1)S(1)} %bitcast.58, bf16[3840,512]{1,0:T(8,128)(2,1)S(1)} %copy-done.7), kind=kOutput, calls=%fused_computation.56 | convolution fusion | flops 1509949440 | bytes 10223616 | tf_op jit(solution)/shard_map/dot_general | solution.py:23
  255.3 13.9 %collective-permute-done.13 = bf16[384,1024]{1,0:T(8,128)(2,1)} collective-permute-done((bf16[384,1024]{1,0:T(8,128)(2,1)}, bf16[384,1024]{1,0:T(8,128)(2,1)}, u32[]{:S(2)}, u32[]{:S(2)}) %collective-permute-start.13) | collective-permute-done | bytes 786464 | tf_op jit(solution)/shard_map/ppermute | solution.py:29
  270.5 5.5 %collective-permute-done.11 = bf16[384,1024]{1,0:T(8,128)(2,1)} collective-permute-done((bf16[384,1024]{1,0:T(8,128)(2,1)}, bf16[384,1024]{1,0:T(8,128)(2,1)}, u32[]{:S(2)}, u32[]{:S(2)}) %collective-permute-start.11) | collective-permute-done | bytes 786464 | tf_op jit(solution)/shard_map/ppermute | solution.py:29
  276.0 12.0 %collective-permute-start.12 = (bf16[384,1024]{1,0:T(8,128)(2,1)}, bf16[384,1024]{1,0:T(8,128)(2,1)}, u32[]{:S(2)}, u32[]{:S(2)}) collective-permute-start(bf16[384,1024]{1,0:T(8,128)(2,1)} %collective-permute-done.11), channel_id=1, source_target_pairs={{0,8},{4,12},{8,16},{12,20},{16,24},{20,28},{1,9},{5,13},{9,17},{1... | collective-permute-start | bytes 2359304 | tf_op jit(solution)/shard_map/ppermute | solution.py:29
  287.9 8.7 %add_convert_fusion = bf16[384,3840]{1,0:T(8,128)(2,1)S(1)} fusion(f32[384,3840]{1,0:T(8,128)} %fusion.15, f32[384,3840]{1,0:T(8,128)S(1)} %fusion.14, bf16[384,1024]{1,0:T(8,128)(2,1)} %get-tuple-element.12, bf16[3840,1024]{1,0:T(8,128)(2,1)} %param.9), kind=kOutput, calls=%fused_computation | convolution fusion | flops 3024322560 | bytes 23396352 | tf_op jit(solution)/shard_map/dot_general | solution.py:23
  307.0 13.2 %collective-permute-done.15 = bf16[384,1024]{1,0:T(8,128)(2,1)S(1)} collective-permute-done((bf16[384,1024]{1,0:T(8,128)(2,1)}, bf16[384,1024]{1,0:T(8,128)(2,1)S(1)}, u32[]{:S(2)}, u32[]{:S(2)}) %collective-permute-start.15) | collective-permute-done | bytes 786464 | tf_op jit(solution)/shard_map/ppermute | solution.py:29
  324.3 5.8 %collective-permute-done.8 = bf16[96,3840]{1,0:T(8,128)(2,1)S(1)} collective-permute-done((bf16[96,3840]{1,0:T(8,128)(2,1)S(1)}, bf16[96,3840]{1,0:T(8,128)(2,1)S(1)}, u32[]{:S(2)}, u32[]{:S(2)}) %collective-permute-start.8) | collective-permute-done | bytes 737312 | tf_op jit(solution)/shard_map/ppermute | solution.py:198
  331.3 4.2 %convolution_convert_fusion = bf16[480,1024]{1,0:T(8,128)(2,1)S(1)} fusion(bf16[1536,480]{0,1:T(8,128)(2,1)} %copy-done.15, bf16[1536,1024]{1,0:T(8,128)(2,1)} %all-gather.8.cloned.1.call-done), kind=kOutput, calls=%fused_computation.14 | convolution fusion | flops 1510440960 | bytes 5603328 | tf_op jit(solution)/shard_map/dot_general | solution.py:23
  335.6 13.7 %collective-permute-done.16 = bf16[480,1024]{1,0:T(8,128)(2,1)} collective-permute-done((bf16[480,1024]{1,0:T(8,128)(2,1)}, bf16[480,1024]{1,0:T(8,128)(2,1)}, u32[]{:S(2)}, u32[]{:S(2)}) %collective-permute-start.16) | collective-permute-done | bytes 983072 | tf_op jit(solution)/shard_map/ppermute | solution.py:254
  349.3 4.4 %add_convert_fusion.1 = bf16[480,1024]{1,0:T(8,128)(2,1)S(1)} fusion(bf16[480,1024]{1,0:T(8,128)(2,1)} %collective-permute-done.16, bf16[2688,1024]{1,0:T(8,128)(2,1)S(1)} %copy-done.18, s32[]{:T(128)S(6)} %select_n.30, bf16[1536,480]{0,1:T(8,128)(2,1)S(1)} %copy-done.14), kind=kOutput, calls=%fused_computation.5 | convolution fusion | flops 2643886080 | bytes 8945668 | tf_op jit(solution)/shard_map/dot_general | solution.py:23
  354.7 12.8 %collective-permute-done.9 = bf16[480,1024]{1,0:T(8,128)(2,1)S(1)} collective-permute-done((bf16[480,1024]{1,0:T(8,128)(2,1)S(1)}, bf16[480,1024]{1,0:T(8,128)(2,1)S(1)}, u32[]{:S(2)}, u32[]{:S(2)}) %collective-permute-start.9) | collective-permute-done | bytes 983072 | tf_op jit(solution)/shard_map/ppermute | solution.py:254
  (129 shorter events, 61.3 us)
Async XLA Ops:
  7.2 32.6 %all-gather.4.cloned.1.call-start = ((), (), s32[]{:S(2)}) async-start(), calls=%async_computation.1 | async-start | bytes 3686400 | tf_op jit(solution)/shard_map/all_gather | solution.py:204
  11.7 26.4 %all-to-all-start = ((bf16[4,96,960]{2,1,0:T(8,128)(2,1)}), bf16[4,96,960]{2,1,0:T(8,128)(2,1)S(1)}, u32[]{:S(2)}, u32[]{:S(2)}) async-start(bf16[4,96,960]{2,1,0:T(8,128)(2,1)} %copy.35), calls=%async_computation | async-start | bytes 1572864 | tf_op jit(solution)/shard_map/all_to_all | solution.py:238
  18.0 165.8 %all-gather.6.cloned.1.call-start = ((), (), s32[]{:S(2)}) async-start(), calls=%async_computation.2 | async-start | bytes 3932160 | tf_op jit(solution)/shard_map/all_gather | solution.py:245
  39.6 291.7 %all-gather.8.cloned.1.call-start = ((), (), s32[]{:S(2)}) async-start(), calls=%async_computation.3 | async-start | bytes 3932160 | tf_op jit(solution)/shard_map/all_gather | solution.py:265
  53.0 31.7 %collective-permute-start.1 = (bf16[384,1024]{1,0:T(8,128)(2,1)S(1)}, bf16[384,1024]{1,0:T(8,128)(2,1)S(1)}, u32[]{:S(2)}, u32[]{:S(2)}) collective-permute-start(bf16[384,1024]{1,0:T(8,128)(2,1)S(1)} %bitcast.53), channel_id=1, source_target_pairs={{0,8},{4,12},{8,16},{12,20},{16,24},{20,28},{1,9},{5,13},{9,17},{1... | collective-permute-start | bytes 2359304 | tf_op jit(solution)/shard_map/ppermute | solution.py:29
  56.3 28.4 %collective-permute-start.2 = (bf16[384,1024]{1,0:T(8,128)(2,1)S(1)}, bf16[384,1024]{1,0:T(8,128)(2,1)S(1)}, u32[]{:S(2)}, u32[]{:S(2)}) collective-permute-start(bf16[384,1024]{1,0:T(8,128)(2,1)S(1)} %bitcast.54), channel_id=1, source_target_pairs={{0,4},{4,8},{8,12},{12,16},{16,20},{20,24},{24,28},{1,5},{5,9},{9,... | collective-permute-start | bytes 2359304 | tf_op jit(solution)/shard_map/ppermute | solution.py:29
  60.2 24.5 %collective-permute-start = (bf16[256,1024]{1,0:T(8,128)(2,1)S(1)}, bf16[256,1024]{1,0:T(8,128)(2,1)S(1)}, u32[]{:S(2)}, u32[]{:S(2)}) collective-permute-start(bf16[256,1024]{1,0:T(8,128)(2,1)S(1)} %bitcast.74), channel_id=1, source_target_pairs={{0,12},{4,16},{8,20},{12,24},{16,28},{1,13},{5,17},{9,21},{13,25},... | collective-permute-start | bytes 1572872 | tf_op jit(solution)/shard_map/ppermute | solution.py:29
  98.6 62.7 %collective-permute-start.3 = (bf16[384,1024]{1,0:T(8,128)(2,1)}, bf16[384,1024]{1,0:T(8,128)(2,1)}, u32[]{:S(2)}, u32[]{:S(2)}) collective-permute-start(bf16[384,1024]{1,0:T(8,128)(2,1)} %get-tuple-element.14), channel_id=1, source_target_pairs={{4,0},{8,4},{12,8},{16,12},{20,16},{24,20},{28,24},{5,1},{9,5},{13... | collective-permute-start | bytes 2359304 | tf_op jit(solution)/shard_map/ppermute | solution.py:29
  99.9 61.5 %collective-permute-start.4 = (bf16[384,1024]{1,0:T(8,128)(2,1)S(1)}, bf16[384,1024]{1,0:T(8,128)(2,1)}, u32[]{:S(2)}, u32[]{:S(2)}) collective-permute-start(bf16[384,1024]{1,0:T(8,128)(2,1)S(1)} %get-tuple-element.15), channel_id=1, source_target_pairs={{8,0},{12,4},{16,8},{20,12},{24,16},{28,20},{9,1},{13,5},{17,9},{2... | collective-permute-start | bytes 2359304 | tf_op jit(solution)/shard_map/ppermute | solution.py:29
  101.2 60.2 %collective-permute-start.5 = (bf16[256,1024]{1,0:T(8,128)(2,1)S(1)}, bf16[256,1024]{1,0:T(8,128)(2,1)}, u32[]{:S(2)}, u32[]{:S(2)}) collective-permute-start(bf16[256,1024]{1,0:T(8,128)(2,1)S(1)} %get-tuple-element.16), channel_id=1, source_target_pairs={{12,0},{16,4},{20,8},{24,12},{28,16},{13,1},{17,5},{21,9},{25,13},... | collective-permute-start | bytes 1572872 | tf_op jit(solution)/shard_map/ppermute | solution.py:29
  172.5 25.9 %collective-permute-start.10 = (bf16[384,1024]{1,0:T(8,128)(2,1)}, bf16[384,1024]{1,0:T(8,128)(2,1)}, u32[]{:S(2)}, u32[]{:S(2)}) collective-permute-start(bf16[384,1024]{1,0:T(8,128)(2,1)} %pad_maximum_fusion.2), channel_id=1, source_target_pairs={{0,8},{4,12},{8,16},{12,20},{16,24},{20,28},{1,9},{5,13},{9,17},{1... | collective-permute-start | bytes 2359304 | tf_op jit(solution)/shard_map/ppermute | solution.py:29
  195.4 53.8 %copy-start.5 = (bf16[384,512]{1,0:T(8,128)(2,1)S(1)}, bf16[384,512]{1,0:T(8,128)(2,1)}, u32[]{:S(2)}) copy-start(bf16[384,512]{1,0:T(8,128)(2,1)} %copy-done.4) | copy-start | bytes 1179652
  196.8 123.5 %copy-start.15 = (bf16[1536,480]{0,1:T(8,128)(2,1)}, bf16[1536,480]{0,1:T(8,128)(2,1)S(1)}, u32[]{:S(2)}) copy-start(bf16[1536,480]{0,1:T(8,128)(2,1)S(1)} %get-tuple-element.18) | copy-start | bytes 4423684
  196.8 54.2 %copy-start.7 = (bf16[3840,512]{1,0:T(8,128)(2,1)S(1)}, bf16[3840,512]{1,0:T(8,128)(2,1)}, u32[]{:S(2)}) copy-start(bf16[3840,512]{1,0:T(8,128)(2,1)} %param.11) | copy-start | bytes 11796484
  196.8 72.4 %collective-permute-start.13 = (bf16[384,1024]{1,0:T(8,128)(2,1)}, bf16[384,1024]{1,0:T(8,128)(2,1)}, u32[]{:S(2)}, u32[]{:S(2)}) collective-permute-start(bf16[384,1024]{1,0:T(8,128)(2,1)} %pad_maximum_fusion.2), channel_id=1, source_target_pairs={{8,0},{12,4},{16,8},{20,12},{24,16},{28,20},{9,1},{13,5},{17,9},{2... | collective-permute-start | bytes 2359304 | tf_op jit(solution)/shard_map/ppermute | solution.py:29
  198.3 77.6 %collective-permute-start.11 = (bf16[384,1024]{1,0:T(8,128)(2,1)}, bf16[384,1024]{1,0:T(8,128)(2,1)}, u32[]{:S(2)}, u32[]{:S(2)}) collective-permute-start(bf16[384,1024]{1,0:T(8,128)(2,1)} %collective-permute-done.10), channel_id=1, source_target_pairs={{0,8},{4,12},{8,16},{12,20},{16,24},{20,28},{1,9},{5,13},{9,17},{1... | collective-permute-start | bytes 2359304 | tf_op jit(solution)/shard_map/ppermute | solution.py:29
  269.2 30.2 %collective-permute-start.14 = (bf16[384,1024]{1,0:T(8,128)(2,1)}, bf16[384,1024]{1,0:T(8,128)(2,1)}, u32[]{:S(2)}, u32[]{:S(2)}) collective-permute-start(bf16[384,1024]{1,0:T(8,128)(2,1)} %collective-permute-done.13), channel_id=1, source_target_pairs={{8,0},{12,4},{16,8},{20,12},{24,16},{28,20},{9,1},{13,5},{17,9},{2... | collective-permute-start | bytes 2359304 | tf_op jit(solution)/shard_map/ppermute | solution.py:29
  276.0 25.0 %collective-permute-start.12 = (bf16[384,1024]{1,0:T(8,128)(2,1)}, bf16[384,1024]{1,0:T(8,128)(2,1)}, u32[]{:S(2)}, u32[]{:S(2)}) collective-permute-start(bf16[384,1024]{1,0:T(8,128)(2,1)} %collective-permute-done.11), channel_id=1, source_target_pairs={{0,8},{4,12},{8,16},{12,20},{16,24},{20,28},{1,9},{5,13},{9,17},{1... | collective-permute-start | bytes 2359304 | tf_op jit(solution)/shard_map/ppermute | solution.py:29
  296.7 27.5 %collective-permute-start.6 = (bf16[96,3840]{1,0:T(8,128)(2,1)S(1)}, bf16[96,3840]{1,0:T(8,128)(2,1)S(1)}, u32[]{:S(2)}, u32[]{:S(2)}) collective-permute-start(bf16[96,3840]{1,0:T(8,128)(2,1)S(1)} %get-tuple-element.19), channel_id=1, source_target_pairs={{0,1},{1,2},{2,3},{3,0},{4,5},{5,6},{6,7},{7,4},{8,9},{9,10},{10,1... | collective-permute-start | bytes 2211848 | tf_op jit(solution)/shard_map/ppermute | solution.py:198
  296.8 27.4 %collective-permute-start.7 = (bf16[96,3840]{1,0:T(8,128)(2,1)S(1)}, bf16[96,3840]{1,0:T(8,128)(2,1)S(1)}, u32[]{:S(2)}, u32[]{:S(2)}) collective-permute-start(bf16[96,3840]{1,0:T(8,128)(2,1)S(1)} %get-tuple-element.21), channel_id=1, source_target_pairs={{0,2},{1,3},{2,0},{3,1},{4,6},{5,7},{6,4},{7,5},{8,10},{9,11},{10,... | collective-permute-start | bytes 2211848 | tf_op jit(solution)/shard_map/ppermute | solution.py:198
  298.0 32.0 %collective-permute-start.8 = (bf16[96,3840]{1,0:T(8,128)(2,1)S(1)}, bf16[96,3840]{1,0:T(8,128)(2,1)S(1)}, u32[]{:S(2)}, u32[]{:S(2)}) collective-permute-start(bf16[96,3840]{1,0:T(8,128)(2,1)S(1)} %get-tuple-element.20), channel_id=1, source_target_pairs={{0,3},{1,0},{2,1},{3,2},{4,7},{5,4},{6,5},{7,6},{8,11},{9,8},{10,9... | collective-permute-start | bytes 2211848 | tf_op jit(solution)/shard_map/ppermute | solution.py:198
  299.4 20.8 %collective-permute-start.15 = (bf16[384,1024]{1,0:T(8,128)(2,1)}, bf16[384,1024]{1,0:T(8,128)(2,1)S(1)}, u32[]{:S(2)}, u32[]{:S(2)}) collective-permute-start(bf16[384,1024]{1,0:T(8,128)(2,1)} %collective-permute-done.14), channel_id=1, source_target_pairs={{8,0},{12,4},{16,8},{20,12},{24,16},{28,20},{9,1},{13,5},{17,9},{2... | collective-permute-start | bytes 2359304 | tf_op jit(solution)/shard_map/ppermute | solution.py:29
  324.2 25.0 %collective-permute-start.16 = (bf16[480,1024]{1,0:T(8,128)(2,1)}, bf16[480,1024]{1,0:T(8,128)(2,1)}, u32[]{:S(2)}, u32[]{:S(2)}) collective-permute-start(bf16[480,1024]{1,0:T(8,128)(2,1)} %fusion.5), channel_id=1, source_target_pairs={{0,4},{4,0},{8,12},{12,8},{16,20},{20,16},{24,28},{28,24},{1,5},{5... | collective-permute-start | bytes 2949128 | tf_op jit(solution)/shard_map/ppermute | solution.py:254
  335.5 32.0 %collective-permute-start.9 = (bf16[480,1024]{1,0:T(8,128)(2,1)S(1)}, bf16[480,1024]{1,0:T(8,128)(2,1)S(1)}, u32[]{:S(2)}, u32[]{:S(2)}) collective-permute-start(bf16[480,1024]{1,0:T(8,128)(2,1)S(1)} %convolution_convert_fusion), channel_id=1, source_target_pairs={{0,4},{4,0},{8,12},{12,8},{16,20},{20,16},{24,28},{28,24},{1,5},{5... | collective-permute-start | bytes 2949128 | tf_op jit(solution)/shard_map/ppermute | solution.py:254
  (20 other events, 237.1 us)
Sparse Core Ops, SparseCore 0:
  9.6 30.1 all-gather.3
  41.3 28.5 all-gather.5
  183.9 97.0 all-gather.7
